TPU v7x, 32 devices: a whole 2x2x4 slice. The times are simulated.
32 devices in a mesh: slab: 8 (over z, x), freq: 4 (over y, core).
Axes of the slice: x: 2, y: 2, z: 4, core: 2. Of those that a mesh axis runs over, the one named last changes fastest.
Arguments:
- source: bfloat16 [4, 2, 3, 64, 64, 128], P('freq', None, None, 'slab'), may hold values from -6 to 6
- omega: float32 [4], P('freq'), may hold values from 0.2 to 5
- sigma_blocks: float32 [256], replicated, may hold values from 0.25 to 4
- block_ids: int32 [64, 64, 128], P('slab'), may hold values from 0 to 255
- rec_owner: int32 [1024, 1], P('slab'), may hold values from 0 to 7; in each aligned block of 128 rows (0 to 127, 128 to 255, ...) at most 32 rows name the same one
- rec_edge: int32 [1024], P('slab'), may hold values from 0 to 196607
- observed: float32 [4, 2, 1024], P('freq', None, 'slab'), may hold values from -4 to 4
Outputs:
- forward_field: float32 [4, 2, 3, 64, 64, 128], P('freq', None, None, 'slab')
- adjoint_field: float32 [4, 2, 3, 64, 64, 128], P('freq', None, None, 'slab')
- gradient: float32 [256], replicated
Inputs may be any that keep to these rules, and one draw needn't show every extreme that they name: `rec_owner`: among the receiver rows of one slab device no slab is named more than 32 times; in some device's rows one slab is named exactly 32 times.
All inputs are finite; a program needn't handle non-finite values.
Results may differ from a plain program's by a relative error of at most 0.0003.
Values sent between devices are 32-bit elements; how exact they have to be, the bound alone decides.
A program may use at most 256 MiB of HBM per device.

v0:
```python
import jax
import jax.numpy as jnp
from jax import lax
from jax.sharding import PartitionSpec as P

SWEEPS = 4


epsilon = 1e-06


def extended(cells, sides, width):
    for axis, dim in sides:
        count = lax.axis_size(axis)
        ends = count - 1
        head = lax.slice_in_dim(cells, 0, width, axis=dim)
        tail = lax.slice_in_dim(cells, cells.shape[dim] - width, cells.shape[dim], axis=dim)
        cells = jnp.concatenate(
            [
                lax.ppermute(tail, axis, [(i, (i + 1) % count) for i in range(ends)]),
                cells,
                lax.ppermute(head, axis, [((i + 1) % count, i) for i in range(ends)]),
            ],
            axis=dim,
        )
    return cells


def forward_diff(values, along):
    along = along % values.ndim
    count = values.shape[along]
    ahead_values = jnp.concatenate(
        [
            lax.slice_in_dim(values, 1, count, axis=along),
            jnp.zeros_like(lax.slice_in_dim(values, 0, 1, axis=along)),
        ],
        axis=along,
    )
    return ahead_values - values


def adjoint_diff(values, along):
    along = along % values.ndim
    count = values.shape[along]
    behind = jnp.concatenate(
        [
            jnp.zeros_like(lax.slice_in_dim(values, 0, 1, axis=along)),
            lax.slice_in_dim(values, 0, count - 1, axis=along),
        ],
        axis=along,
    )
    return behind - values


def stiffness_of(field):
    padded = extended(field, (("slab", 3),), 1)
    edge_first = padded[:, :, 0]
    edge_second = padded[:, :, 1]
    edge_third = padded[:, :, 2]
    curl_first = forward_diff(edge_third[:, :, 1:-1], -2) - forward_diff(
        edge_second[:, :, 1:-1], -1
    )
    full_second = forward_diff(edge_first[:, :, :-1], -1) - (
        edge_third[:, :, 1:] - edge_third[:, :, :-1]
    )
    full_third = (
        edge_second[:, :, 1:] - edge_second[:, :, :-1] - forward_diff(edge_first[:, :, :-1], -2)
    )
    lower_valid = (lax.axis_index("slab") > 0).astype(jnp.float32)
    curl_second = jnp.concatenate(
        [full_second[:, :, :1] * lower_valid, full_second[:, :, 1:]], axis=2
    )
    curl_third = jnp.concatenate([full_third[:, :, :1] * lower_valid, full_third[:, :, 1:]], axis=2)
    back_first = adjoint_diff(curl_second[:, :, 1:], -1) - adjoint_diff(curl_third[:, :, 1:], -2)
    back_second = curl_third[:, :, :-1] - curl_third[:, :, 1:] - adjoint_diff(curl_first, -1)
    back_third = adjoint_diff(curl_first, -2) - (curl_second[:, :, :-1] - curl_second[:, :, 1:])
    return jnp.stack([back_first, back_second, back_third], axis=2)


def residual_sweeps(right_side, damping):
    denominator = 16.0 + damping * damping
    residual = right_side
    solution = jnp.zeros_like(right_side)
    for iteration in range(SWEEPS):
        residual_real = residual[:, 0]
        residual_imag = residual[:, 1]
        precond_real = (4.0 * residual_real + damping * residual_imag) / denominator
        precond_imag = (4.0 * residual_imag - damping * residual_real) / denominator
        stiffness = stiffness_of(jnp.stack([precond_real, precond_imag], axis=1))
        image_real = stiffness[:, 0] - damping * precond_imag
        image_imag = stiffness[:, 1] + damping * precond_real
        totals = lax.psum(
            (
                jnp.sum(image_real * residual_real + image_imag * residual_imag, axis=(1, 2, 3, 4)),
                jnp.sum(image_real * residual_imag - image_imag * residual_real, axis=(1, 2, 3, 4)),
                jnp.sum(image_real * image_real + image_imag * image_imag, axis=(1, 2, 3, 4)),
            ),
            "slab",
        )
        lower_sum = totals[2] + epsilon
        step_real = (totals[0] / lower_sum)[:, None, None, None, None]
        step_imag = (totals[1] / lower_sum)[:, None, None, None, None]
        solution = solution + jnp.stack(
            [
                step_real * precond_real - step_imag * precond_imag,
                step_real * precond_imag + step_imag * precond_real,
            ],
            axis=1,
        )
        residual = residual - jnp.stack(
            [
                step_real * image_real - step_imag * image_imag,
                step_real * image_imag + step_imag * image_real,
            ],
            axis=1,
        )
    return solution


def body(source, omega, sigma_blocks, block_ids, rec_owner, rec_edge, observed):
    conductivity = jnp.take(sigma_blocks, block_ids, axis=0)
    damping = omega[:, None, None, None, None] * conductivity[None, None]
    forward_field = residual_sweeps(source.astype(jnp.float32), damping)
    pair_count = forward_field.shape[0]
    flat_field = forward_field.reshape(pair_count, 2, -1)
    slab_count = lax.axis_size("slab")
    owner_slab = rec_owner[:, 0]
    local_count = rec_edge.shape[0]
    owner_hits = (owner_slab[:, None] == jnp.arange(slab_count, dtype=jnp.int32)[None, :]).astype(
        jnp.int32
    )
    earlier = jnp.cumsum(owner_hits, axis=0) - owner_hits
    slot_index = jnp.sum(earlier * owner_hits, axis=1)
    capacity = local_count // 4
    target = owner_slab * capacity + slot_index
    request = (
        jnp.full((slab_count * capacity,), -1, jnp.int32)
        .at[target]
        .set(rec_edge)
        .reshape(slab_count, capacity)
    )
    arrived = lax.all_to_all(request, "slab", split_axis=0, concat_axis=0, tiled=True)
    wanted = arrived.reshape(-1)
    present = (wanted >= 0).astype(jnp.float32)
    safe_edge = jnp.maximum(wanted, 0)
    picked = (jnp.take(flat_field, safe_edge, axis=2) * present).reshape(
        pair_count, 2, slab_count, capacity
    )
    returned = lax.all_to_all(picked, "slab", split_axis=2, concat_axis=2, tiled=True)
    predicted = jnp.take(returned.reshape(pair_count, 2, -1), target, axis=2)
    misfit = predicted - observed
    adjoint_data = jnp.stack([misfit[:, 0], -misfit[:, 1]], axis=1)
    outgoing = (
        jnp.zeros((pair_count, 2, slab_count * capacity), jnp.float32)
        .at[:, :, target]
        .set(adjoint_data)
        .reshape(pair_count, 2, slab_count, capacity)
    )
    incoming = lax.all_to_all(outgoing, "slab", split_axis=2, concat_axis=2, tiled=True)
    adjoint_flat = (
        jnp.zeros_like(flat_field)
        .at[:, :, safe_edge]
        .add(incoming.reshape(pair_count, 2, -1) * present)
    )
    adjoint_field = residual_sweeps(adjoint_flat.reshape(forward_field.shape), damping)
    cell_term = jnp.sum(
        omega[:, None, None, None]
        * jnp.sum(
            adjoint_field[:, 0] * forward_field[:, 1] + adjoint_field[:, 1] * forward_field[:, 0],
            axis=1,
        ),
        axis=0,
    )
    local_terms = jax.ops.segment_sum(
        cell_term.reshape(-1), block_ids.reshape(-1), num_segments=sigma_blocks.shape[0]
    )
    gradient = lax.psum(local_terms, ("slab", "freq"))
    return (forward_field, adjoint_field, gradient)


def solution(mesh):
    return jax.shard_map(
        body,
        mesh=mesh,
        in_specs=(
            P("freq", None, None, "slab", None, None),
            P("freq"),
            P(),
            P("slab", None, None),
            P("slab", None),
            P("slab"),
            P("freq", None, "slab"),
        ),
        out_specs=(
            P("freq", None, None, "slab", None, None),
            P("freq", None, None, "slab", None, None),
            P(),
        ),
        check_vma=False,
    )
```

profile of v0, /device:TPU:0, one launch (start us, length us, event | category | flops | bytes accessed | tf_op | source)
XLA Modules:
  0.0 1428.2 jit_solution(17710169639621398789)
XLA Ops:
  2.8 406.1 %gather_fusion = f32[65536]{0:T(1024)S(1)} fusion(f32[256]{0:T(256)S(1)} %copy-done, s32[65536]{0:T(1024)S(1)} %broadcast_clamp_fusion), kind=kCustom, calls=%fused_computation | custom fusion | bytes 786432 | tf_op jit(solution)/shard_map/jit(_take)/gather | solution.py:121
  412.1 6.2 collective-permute-start
  420.7 4.4 collective-permute-done
  431.1 20.7 %all-reduce.71 = (f32[1]{0:T(128)}, f32[1]{0:T(128)}, f32[1]{0:T(128)}) all-reduce(f32[1]{0:T(128)} %bitcast.16, f32[1]{0:T(128)} %bitcast.14, f32[1]{0:T(128)} %bitcast.13), channel_id=1, replica_groups=mesh['slab'=8,'freq'=4] {'slab'}, use_global_device_ids=true, to_apply=%region_5.6 | all-reduce | flops 3 | bytes 24 | tf_op jit(solution)/shard_map/psum | solution.py:92
  453.5 3.7 multiply_subtract_fusion.12
  461.1 5.2 collective-permute-start.2
  477.8 22.5 %all-reduce.70 = (f32[1]{0:T(128)}, f32[1]{0:T(128)}, f32[1]{0:T(128)}) all-reduce(f32[1]{0:T(128)} %bitcast.32, f32[1]{0:T(128)} %bitcast.30, f32[1]{0:T(128)} %bitcast.29), channel_id=1, replica_groups=mesh['slab'=8,'freq'=4] {'slab'}, use_global_device_ids=true, to_apply=%region_11.12 | all-reduce | flops 3 | bytes 24 | tf_op jit(solution)/shard_map/psum | solution.py:92
  502.2 3.7 multiply_subtract_fusion.10
  509.7 5.4 collective-permute-start.4
  523.7 20.5 %all-reduce.69 = (f32[1]{0:T(128)}, f32[1]{0:T(128)}, f32[1]{0:T(128)}) all-reduce(f32[1]{0:T(128)} %bitcast.48, f32[1]{0:T(128)} %bitcast.46, f32[1]{0:T(128)} %bitcast.45), channel_id=1, replica_groups=mesh['slab'=8,'freq'=4] {'slab'}, use_global_device_ids=true, to_apply=%region_17.18 | all-reduce | flops 3 | bytes 24 | tf_op jit(solution)/shard_map/psum | solution.py:92
  546.1 3.7 multiply_subtract_fusion.8
  552.1 4.6 collective-permute-start.6
  564.2 20.3 %all-reduce.68 = (f32[1]{0:T(128)}, f32[1]{0:T(128)}, f32[1]{0:T(128)}) all-reduce(f32[1]{0:T(128)} %bitcast.64, f32[1]{0:T(128)} %bitcast.62, f32[1]{0:T(128)} %bitcast.61), channel_id=1, replica_groups=mesh['slab'=8,'freq'=4] {'slab'}, use_global_device_ids=true, to_apply=%region_23.24 | all-reduce | flops 3 | bytes 24 | tf_op jit(solution)/shard_map/psum | solution.py:92
  588.8 5.9 fusion.7
  594.7 44.4 %copy.224 = f32[2,196608]{0,1:T(8,128)} copy(f32[2,196608]{1,0:T(2,128)S(1)} %fusion.7) | data formatting | bytes 3145728 | tf_op jit(solution)/shard_map/add | solution.py:103
  639.1 7.6 gather_fusion.1
  647.4 3.7 all-to-all-start.1
  653.7 3.9 all-to-all-done.1
  663.7 6.4 all-to-all-done.2
  670.3 44.8 %scatter_custom_fusion.2 = f32[2,196608]{0,1:T(8,128)} fusion(s32[256]{0:T(256)S(1)} %get-tuple-element.3, f32[]{:T(128)} %constant.38.clone.1, f32[256,2]{1,0:T(8,128)S(1)} %copy.232, s32[1024]{0:T(1024)S(1)} %pad_clamp_fusion), kind=kCustom, calls=%fused_computation.8 | custom fusion | flops 512 | bytes 1572868 | tf_op jit(solution)/shard_map/scatter-add | solution.py:163
  715.1 57.2 %copy.233 = f32[1,2,3,8,64,128]{5,4,3,2,1,0:T(8,128)S(1)} copy(f32[1,2,3,8,64,128]{1,5,4,3,2,0:T(8,128)} %bitcast.92) | data formatting | bytes 3145728 | tf_op jit(solution)/shard_map/reshape | solution.py:165
  773.8 4.6 collective-permute-start.8
  786.5 20.3 %all-reduce.67 = (f32[1]{0:T(128)}, f32[1]{0:T(128)}, f32[1]{0:T(128)}) all-reduce(f32[1]{0:T(128)} %bitcast.106, f32[1]{0:T(128)} %bitcast.104, f32[1]{0:T(128)} %bitcast.103), channel_id=1, replica_groups=mesh['slab'=8,'freq'=4] {'slab'}, use_global_device_ids=true, to_apply=%region_34.35 | all-reduce | flops 3 | bytes 24 | tf_op jit(solution)/shard_map/psum | solution.py:92
  814.7 4.8 collective-permute-start.10
  827.3 20.3 %all-reduce.66 = (f32[1]{0:T(128)}, f32[1]{0:T(128)}, f32[1]{0:T(128)}) all-reduce(f32[1]{0:T(128)} %bitcast.122, f32[1]{0:T(128)} %bitcast.120, f32[1]{0:T(128)} %bitcast.119), channel_id=1, replica_groups=mesh['slab'=8,'freq'=4] {'slab'}, use_global_device_ids=true, to_apply=%region_40.41 | all-reduce | flops 3 | bytes 24 | tf_op jit(solution)/shard_map/psum | solution.py:92
  855.5 4.6 collective-permute-start.12
  861.8 4.3 collective-permute-done.12
  870.8 20.3 %all-reduce.65 = (f32[1]{0:T(128)}, f32[1]{0:T(128)}, f32[1]{0:T(128)}) all-reduce(f32[1]{0:T(128)} %bitcast.138, f32[1]{0:T(128)} %bitcast.136, f32[1]{0:T(128)} %bitcast.135), channel_id=1, replica_groups=mesh['slab'=8,'freq'=4] {'slab'}, use_global_device_ids=true, to_apply=%region_46.47 | all-reduce | flops 3 | bytes 24 | tf_op jit(solution)/shard_map/psum | solution.py:92
  899.1 4.8 collective-permute-start.14
  911.1 20.3 %all-reduce.64 = (f32[1]{0:T(128)}, f32[1]{0:T(128)}, f32[1]{0:T(128)}) all-reduce(f32[1]{0:T(128)} %bitcast.154, f32[1]{0:T(128)} %bitcast.152, f32[1]{0:T(128)} %bitcast.151), channel_id=1, replica_groups=mesh['slab'=8,'freq'=4] {'slab'}, use_global_device_ids=true, to_apply=%region_52.53 | all-reduce | flops 3 | bytes 24 | tf_op jit(solution)/shard_map/psum | solution.py:92
  938.2 452.6 %scatter_custom_fusion.3 = f32[256]{0:T(256)S(1)} fusion(s32[65536]{0:T(1024)} %bitcast.724, f32[65536]{0:T(1024)S(1)} %bitcast.727, f32[]{:T(128)} %constant.38.clone.1), kind=kCustom, calls=%fused_computation.483 | custom fusion | flops 65536 | bytes 1536 | tf_op jit(solution)/shard_map/scatter-add | solution.py:174
  1390.8 36.9 %psum.199 = f32[256]{0:T(256)} all-reduce(f32[256]{0:T(256)S(1)} %scatter_custom_fusion.3), channel_id=1, replica_groups=mesh['slab'=8,'freq'=4] {'slab','freq'}, use_global_device_ids=true, to_apply=%region_55.56 | all-reduce | flops 256 | bytes 2048 | tf_op jit(solution)/shard_map/psum | solution.py:177
  (350 shorter events, 115.6 us)
Async XLA Ops:
  409.2 17.2 %copy-start.9 = (f32[1,1,3,8,64,128]{5,4,3,2,1,0:T(8,128)}, f32[1,1,3,8,64,128]{5,4,3,2,1,0:T(8,128)S(1)}, u32[]{:S(2)}) copy-start(f32[1,1,3,8,64,128]{5,4,3,2,1,0:T(8,128)S(1)} %get-tuple-element.99) | copy-start | bytes 2359300
  409.2 9.0 copy-start.61
  410.8 9.9 collective-permute-start.1
  412.1 13.0 collective-permute-start
  459.8 11.7 collective-permute-start.3
  461.1 10.4 collective-permute-start.2
  468.1 47.1 %all-to-all-start = ((s32[8,1,32]{2,1,0:T(1,128)}), s32[8,1,32]{2,1,0:T(1,128)S(1)}, u32[]{:S(2)}, u32[]{:S(2)}) async-start(s32[8,1,32]{2,1,0:T(1,128)} %all_to_all.12), calls=%async_computation | async-start | bytes 8192 | tf_op jit(solution)/shard_map/all_to_all | solution.py:142
  508.4 7.6 collective-permute-start.5
  509.7 7.7 collective-permute-start.4
  550.8 7.7 collective-permute-start.7
  552.1 7.8 collective-permute-start.6
  562.9 24.9 %copy-start.50 = (f32[1,1,3,8,64,128]{5,4,3,2,1,0:T(8,128)S(1)}, f32[1,1,3,8,64,128]{5,4,3,2,1,0:T(8,128)}, u32[]{:S(2)}) copy-start(f32[1,1,3,8,64,128]{5,4,3,2,1,0:T(8,128)} %get-tuple-element.145) | copy-start | bytes 2359300
  594.7 63.8 %copy-start.62 = (f32[1,2,128]{2,1,0:T(2,128)S(1)}, f32[1,2,128]{2,1,0:T(2,128)}, u32[]{:S(2)}) copy-start(f32[1,2,128]{2,1,0:T(2,128)} %param.13) | copy-start | bytes 3076
  647.4 10.2 all-to-all-start.1
  660.2 9.8 all-to-all-start.2
  772.5 9.2 copy-start.17
  772.5 7.6 collective-permute-start.9
  773.8 7.7 collective-permute-start.8
  813.3 9.2 copy-start.15
  813.4 7.6 collective-permute-start.11
  814.7 7.7 collective-permute-start.10
  854.2 12.1 copy-start.16
  854.2 7.6 collective-permute-start.13
  855.5 10.5 collective-permute-start.12
  896.5 7.5 copy-start.52
  897.2 6.8 copy-start.43
  897.2 6.8 copy-start.45
  897.2 6.8 copy-start.47
  897.6 8.3 collective-permute-start.15
  899.1 7.7 collective-permute-start.14
  909.7 23.8 %copy-start.59 = (f32[1,1,3,8,64,128]{5,4,3,2,1,0:T(8,128)S(1)}, f32[1,1,3,8,64,128]{5,4,3,2,1,0:T(8,128)}, u32[]{:S(2)}) copy-start(f32[1,1,3,8,64,128]{5,4,3,2,1,0:T(8,128)} %get-tuple-element.129) | copy-start | bytes 2359300
  935.1 492.6 %copy-start.1 = (f32[256]{0:T(256)S(1)}, f32[256]{0:T(256)}, u32[]{:S(2)}) copy-start(f32[256]{0:T(256)} %param.9) | copy-start | bytes 3076
  (50 other events, 115.9 us)
where the time goes:
time: 1440 us; the launch traced here: 1430 us
  other arithmetic  570 us (40%)
  local copies, waits for them, and re-layouts  542 us (38%)
  blocking collectives  202 us (14%)
  starting transfers between devices  61 us (4%)
  waiting for transfers between devices  35.1 us (2%)
  between operations  18.4 us (1%)
    scatter-add x1, other arithmetic, body(): jax.ops.segment_sum(cell_term.reshape(-1), block_ids.reshape(-1), num_seg...  453 us
    gather x1, local copies, waits for them, and re-layouts, body(): conductivity = jnp.take(sigma_blocks, block_ids, axis=0)  406 us
    psum x8, blocking collectives, residual_sweeps(): lax.psum((jnp.sum(image_real * residual_real + image_imag * residual_imag...  165 us
    reshape x1, local copies, waits for them, and re-layouts, body(): adjoint_flat.reshape(forward_field.shape)  57.2 us
    scatter-add x3, other arithmetic, body(): adjoint_flat = jnp.zeros_like(flat_field).at[:, :, safe_edge].add(incomin...  47.4 us
    add x1, local copies, waits for them, and re-layouts, residual_sweeps(): solution + jnp.stack([step_real * precond_real - step_imag * precond_imag...  44.4 us
    ppermute x8, starting transfers between devices, extended(): lax.ppermute(tail, axis, [(i, (i + 1) % count) for i in range(ends)])  40.1 us
    psum x1, blocking collectives, body(): gradient = lax.psum(local_terms, ('slab', 'freq'))  36.9 us
  transfers between devices with their start and end apart: 19, of which 15 were waited for; matrix products, arithmetic and copies ran while one was open for 1% of the time, Pallas kernels for 0%

commit v1 on v0

v1 whole, which is shorter than its diff:
```python
import functools

import jax
import jax.numpy as jnp
from jax import lax
from jax.experimental import pallas as pl
from jax.experimental.pallas import tpu as pltpu
from jax.sharding import PartitionSpec as P

SWEEPS = 4
EPSILON = 1e-06
LOW = 16
MESH = pl.DeviceIdType.MESH
F32 = jnp.float32
BF16 = jnp.bfloat16
PAIRS = [(i, j) for i in range(SWEEPS + 1) for j in range(i, SWEEPS + 1) if j > 0]


def lookup_kernel(omega_ref, sigma_ref, ids_ref, real_ref, imag_ref):
    planes, rows, lanes = ids_ref.shape
    tables = [jnp.broadcast_to(sigma_ref[k : k + 1, :], (8, lanes)) for k in range(sigma_ref.shape[0])]
    omega = omega_ref[0]
    per = rows // 8

    def step(i, carry):
        x, y = i // per, pl.multiple_of(i % per * 8, 8)
        ids = ids_ref[x, pl.ds(y, 8), :]
        low, high = ids & (lanes - 1), ids >> 7
        value = jnp.take_along_axis(tables[0], low, axis=1)
        for k in range(1, len(tables)):
            value = jnp.where(high == k, jnp.take_along_axis(tables[k], low, axis=1), value)
        damping = omega * value
        inverse = 1.0 / (16.0 + damping * damping)
        real_ref[x, pl.ds(y, 8), :] = 4.0 * inverse
        imag_ref[x, pl.ds(y, 8), :] = damping * inverse
        return carry

    lax.fori_loop(0, planes * per, step, 0, unroll=4)


def split(values):
    high = values.astype(BF16)
    return high, (values - high.astype(F32)).astype(BF16)


def kernel(
    n, nf, high_blocks,
    omega_ref, source_ref, real_ref, imag_ref, ids_ref, pack_ref,
    forward_ref, adjoint_ref, gradient_ref,
    basis, zb, curl, up_out, down_out, low_in, high_in,
    gram_out, gram_in, pack_in, grad_out, grad_in, grad_out2, grad_in2,
    rows_hot, rows_hot_t, field_hi, field_lo, mis_hi, mis_lo, acc,
    up_s, up_r, down_s, down_r, gram_s, gram_r, pack_s, pack_r, grad_s, grad_r, grad2_s, grad2_r,
):
    me = lax.axis_index("slab")
    mine = lax.axis_index("freq")
    planes, rows, lanes = real_ref.shape
    last = planes - 1
    cells_rows = 3 * planes * rows

    barrier = pltpu.get_barrier_semaphore()
    for d in range(1, n):
        pl.semaphore_signal(barrier, inc=1, device_id={"slab": lax.rem(me + d, n)}, device_id_type=MESH)
    for d in range(1, nf):
        pl.semaphore_signal(barrier, inc=1, device_id={"freq": lax.rem(mine + d, nf)}, device_id_type=MESH)
    pl.semaphore_wait(barrier, n + nf - 2)

    def spread(src, dst, send, recv, axis, count, position):
        copies = []
        for d in range(1, count):
            copy = pltpu.make_async_remote_copy(
                src_ref=src, dst_ref=dst.at[d], send_sem=send.at[d], recv_sem=recv.at[d],
                device_id={axis: lax.rem(position + d, count)}, device_id_type=MESH,
            )
            copy.start()
            copies.append(copy)
        return copies

    def total_of(own, buffer, count, position):
        buffer[0] = own
        total = jnp.zeros(own.shape, F32)
        for p in range(count):
            total = total + buffer[lax.rem(position - p + count, count)]
        return total

    lane = lax.broadcasted_iota(jnp.int32, (rows, lanes), 1)
    row = lax.broadcasted_iota(jnp.int32, (rows, lanes), 0)

    def f3(v):
        return jnp.where(lane == lanes - 1, 0.0, pltpu.roll(v, lanes - 1, 1)) - v

    def g3(v):
        return jnp.where(lane == 0, 0.0, pltpu.roll(v, 1, 1)) - v

    def f2(v):
        return jnp.where(row == rows - 1, 0.0, pltpu.roll(v, rows - 1, 0)) - v

    def g2(v):
        return jnp.where(row == 0, 0.0, pltpu.roll(v, 1, 0)) - v

    packs = spread(pack_ref, pack_in, pack_s, pack_r, "slab", n, me)
    pack_in[0] = pack_ref[...]
    valid = jnp.where(me > 0, 1.0, 0.0).astype(F32)

    def precondition(t, x):
        mr, mi = real_ref[x], imag_ref[x]
        for comp in range(3):
            br, bi = basis[t, 0, comp, x], basis[t, 1, comp, x]
            zb[0, comp, x] = mr * br + mi * bi
            zb[1, comp, x] = mr * bi - mi * br

    def up_copy(slot):
        return pltpu.make_async_remote_copy(
            src_ref=up_out.at[slot], dst_ref=low_in.at[slot], send_sem=up_s.at[slot],
            recv_sem=up_r.at[slot], device_id={"slab": lax.rem(me + 1, n)}, device_id_type=MESH,
        )

    def down_copy(slot):
        return pltpu.make_async_remote_copy(
            src_ref=down_out.at[slot], dst_ref=high_in.at[slot], send_sem=down_s.at[slot],
            recv_sem=down_r.at[slot], device_id={"slab": lax.rem(me + n - 1, n)}, device_id_type=MESH,
        )

    def plane(t, c, x, e2n, e3n, b2p, b3p):
        e1, e2, e3 = zb[c, 0, x], zb[c, 1, x], zb[c, 2, x]
        b1 = f2(e3) - f3(e2)
        b2 = f3(e1) - (e3n - e3)
        b3 = e2n - e2 - f2(e1)
        curl[c, 0, x], curl[c, 1, x] = b2, b3
        basis[t + 1, c, 0, x] = g3(b2) - g2(b3) - 4.0 * e1 + basis[t, c, 0, x]
        basis[t + 1, c, 1, x] = b3p - b3 - g3(b1) - 4.0 * e2 + basis[t, c, 1, x]
        basis[t + 1, c, 2, x] = g2(b1) - (b2p - b2) - 4.0 * e3 + basis[t, c, 2, x]

    def apply(first, t):
        slot = first + t
        precondition(t, 0)
        for c in range(2):
            down_out[slot, c, 0] = zb[c, 1, 0]
            down_out[slot, c, 1] = zb[c, 2, 0]

        @pl.when(me > 0)
        def _():
            down_copy(slot).start()

        precondition(t, last)
        for c in range(2):
            up_out[slot, c, 0] = f3(zb[c, 0, last]) + zb[c, 2, last]
            up_out[slot, c, 1] = f2(zb[c, 0, last]) + zb[c, 1, last]

        @pl.when(me < n - 1)
        def _():
            up_copy(slot).start()

        def inner(x, carry):
            precondition(t, x)
            return carry

        lax.fori_loop(1, last, inner, 0)
        for c in range(2):
            curl[c, 0, 0] = f3(zb[c, 0, 0]) - (zb[c, 2, 1] - zb[c, 2, 0])
            curl[c, 1, 0] = zb[c, 1, 1] - zb[c, 1, 0] - f2(zb[c, 0, 0])

        def middle(x, carry):
            for c in range(2):
                plane(t, c, x, zb[c, 1, x + 1], zb[c, 2, x + 1], curl[c, 0, x - 1], curl[c, 1, x - 1])
            return carry

        lax.fori_loop(1, last, middle, 0)

        @pl.when(me > 0)
        def _():
            up_copy(slot).wait_recv()
            down_copy(slot).wait_send()

        @pl.when(me == 0)
        def _():
            low_in[slot] = jnp.zeros(low_in.shape[1:], F32)

        for c in range(2):
            plane(
                t, c, 0, zb[c, 1, 1], zb[c, 2, 1],
                (low_in[slot, c, 0] - zb[c, 2, 0]) * valid,
                (zb[c, 1, 0] - low_in[slot, c, 1]) * valid,
            )

        @pl.when(me < n - 1)
        def _():
            down_copy(slot).wait_recv()
            up_copy(slot).wait_send()

        @pl.when(me == n - 1)
        def _():
            high_in[slot] = jnp.zeros(high_in.shape[1:], F32)

        for c in range(2):
            plane(
                t, c, last, high_in[slot, c, 0], high_in[slot, c, 1],
                curl[c, 0, last - 1], curl[c, 1, last - 1],
            )

    per = rows // 8

    def solve(which, out_ref):
        def sweep(t, carry):
            apply(which * SWEEPS, t)
            return carry

        lax.fori_loop(0, SWEEPS, sweep, 0)

        def products(i, sums):
            x, y = i // per, pl.multiple_of(i % per * 8, 8)
            sums = list(sums)
            for comp in range(3):
                re = [basis[k, 0, comp, x, pl.ds(y, 8), :] for k in range(SWEEPS + 1)]
                im = [basis[k, 1, comp, x, pl.ds(y, 8), :] for k in range(SWEEPS + 1)]
                at = 0
                for i_, j_ in PAIRS:
                    sums[at] = sums[at] + (re[i_] * re[j_] + im[i_] * im[j_])
                    at += 1
                    if i_ != j_:
                        sums[at] = sums[at] + (re[i_] * im[j_] - im[i_] * re[j_])
                        at += 1
            return tuple(sums)

        count = gram_out.shape[1]
        zero = jnp.zeros((8, lanes), F32)
        sums = lax.fori_loop(0, planes * per, products, (zero,) * count)
        for k in range(count):
            gram_out[which, k : k + 1, :] = jnp.sum(sums[k], axis=0, keepdims=True)
        copies = spread(gram_out.at[which], gram_in.at[which], gram_s.at[which], gram_r.at[which], "slab", n, me)
        for copy in copies:
            copy.wait()
        total = total_of(gram_out[which], gram_in.at[which], n, me)
        total = jnp.broadcast_to(jnp.sum(total, axis=1, keepdims=True), total.shape)
        gram, at = {}, 0
        for i, j in PAIRS:
            re = total[at : at + 1, :]
            at += 1
            im = jnp.zeros_like(re)
            if i != j:
                im = total[at : at + 1, :]
                at += 1
            gram[i, j] = (re, im)
            gram[j, i] = (re, -im)
        one = jnp.ones((1, lanes), F32)
        none = jnp.zeros((1, lanes), F32)

        def times(a, b):
            return a[0] * b[0] - a[1] * b[1], a[0] * b[1] + a[1] * b[0]

        poly = [(one, none)]
        coef = [(none, none) for _ in range(SWEEPS)]
        for k in range(SWEEPS):
            up = (none, none)
            below = none
            for i in range(k + 1):
                conj = (poly[i][0], -poly[i][1])
                for j in range(k + 1):
                    both = times(conj, poly[j])
                    term = times(both, gram[i + 1, j])
                    up = (up[0] + term[0], up[1] + term[1])
                    below = below + times(both, gram[i + 1, j + 1])[0]
            below = below + EPSILON
            step = (up[0] / below, up[1] / below)
            moved = [times(step, p) for p in poly]
            for i in range(k + 1):
                coef[i] = (coef[i][0] + moved[i][0], coef[i][1] + moved[i][1])
            grown = poly + [(none, none)]
            for i in range(k + 1):
                grown[i + 1] = (grown[i + 1][0] - moved[i][0], grown[i + 1][1] - moved[i][1])
            poly = grown

        wide = [(jnp.broadcast_to(a, (rows, lanes)), jnp.broadcast_to(b, (rows, lanes))) for a, b in coef]

        def combine(x, carry):
            mr, mi = real_ref[x], imag_ref[x]
            for comp in range(3):
                sr = jnp.zeros((rows, lanes), F32)
                si = jnp.zeros((rows, lanes), F32)
                for k in range(SWEEPS):
                    br, bi = basis[k, 0, comp, x], basis[k, 1, comp, x]
                    sr = sr + (wide[k][0] * br - wide[k][1] * bi)
                    si = si + (wide[k][0] * bi + wide[k][1] * br)
                out_ref[0, comp, x] = mr * sr + mi * si
                out_ref[1, comp, x] = mr * si - mi * sr
            return carry

        lax.fori_loop(0, planes, combine, 0)

    def load(x, carry):
        for c in range(2):
            for comp in range(3):
                basis[0, c, comp, x] = source_ref[c, comp, x].astype(F32)
        return carry

    lax.fori_loop(0, planes, load, 0)
    solve(0, forward_ref)

    for copy in packs:
        copy.wait()
    self_id = me.astype(F32)
    blocks = cells_rows // lanes
    for comp in range(3):
        for c in range(2):
            hi, lo = split(forward_ref[c, comp].reshape(planes * rows, lanes))
            where = (slice(comp * planes * rows, (comp + 1) * planes * rows), slice(c * lanes, (c + 1) * lanes))
            field_hi[where] = hi
            field_lo[where] = lo

    lane_sq = lax.broadcasted_iota(jnp.int32, (lanes, lanes), 1).astype(F32)
    row_sq = lax.broadcasted_iota(jnp.int32, (lanes, lanes), 0).astype(F32)

    def receivers(d, carry):
        pack = pack_in[d]
        at = pl.ds(pl.multiple_of(d * lanes, lanes), lanes)
        owned = jnp.where(pack[0:1, :] == self_id, pack[1:2, :], -1.0)
        owned = jnp.concatenate([owned, pack[2:8, :], owned], axis=0)
        column = jnp.concatenate([owned] * (lanes // 8), axis=0).T
        place = column[:, 0:1]
        for k in range(blocks):
            rows_hot[:, k * lanes : (k + 1) * lanes] = jnp.where(
                lane_sq == place - float(k * lanes), 1.0, 0.0
            ).astype(BF16)
            rows_hot_t[k * lanes : (k + 1) * lanes, at] = jnp.where(
                row_sq == owned[0:1, :] - float(k * lanes), 1.0, 0.0
            ).astype(BF16)
        picked = jnp.dot(rows_hot[...], field_hi[...], preferred_element_type=F32)
        picked = picked + jnp.dot(rows_hot[...], field_lo[...], preferred_element_type=F32)
        here = lane_sq == column[:, 1:2]
        re = jnp.where(here, picked[:, :lanes] - column[:, 2:3], 0.0)
        im = jnp.where(here, column[:, 3:4] - picked[:, lanes:], 0.0)
        for part, values in enumerate((re, im)):
            hi, lo = split(values)
            mis_hi[at, part * lanes : (part + 1) * lanes] = hi
            mis_lo[at, part * lanes : (part + 1) * lanes] = lo
        return carry

    lax.fori_loop(0, n, receivers, 0)
    group = 4
    for comp in range(3):
        for x in range(0, planes, group):
            begin = (comp * planes + x) * rows
            hot = rows_hot_t[begin : begin + group * rows, :]
            added = jnp.dot(hot, mis_hi[...], preferred_element_type=F32)
            added = added + jnp.dot(hot, mis_lo[...], preferred_element_type=F32)
            for c in range(2):
                basis[0, c, comp, x : x + group] = added[:, c * lanes : (c + 1) * lanes].reshape(
                    group, rows, lanes
                )

    solve(1, adjoint_ref)

    omega = omega_ref[0]
    high_iota = lax.broadcasted_iota(jnp.int32, (high_blocks, lanes), 0)
    low_iota = lax.broadcasted_iota(jnp.int32, (LOW, lanes), 0)
    acc[...] = jnp.zeros(acc.shape, F32)
    chunks = rows // 16

    def cells(i, carry):
        x, y = i // chunks, pl.multiple_of(i % chunks * 16, 16)
        value = jnp.zeros((16, lanes), F32)
        for comp in range(3):
            fr, fi = forward_ref[0, comp, x, pl.ds(y, 16), :], forward_ref[1, comp, x, pl.ds(y, 16), :]
            ar, ai = adjoint_ref[0, comp, x, pl.ds(y, 16), :], adjoint_ref[1, comp, x, pl.ds(y, 16), :]
            value = value + (ar * fi + ai * fr)
        value = omega * value
        ids = ids_ref[x, pl.ds(y, 16), :]
        high, low = ids >> 4, ids & (LOW - 1)
        hot = jnp.concatenate(
            [jnp.where(high[r : r + 1, :] == high_iota, 1.0, 0.0) for r in range(16)], axis=0
        ).astype(BF16)
        spot = jnp.concatenate(
            [jnp.where(low[r : r + 1, :] == low_iota, value[r : r + 1, :], 0.0) for r in range(16)], axis=0
        )
        for piece in split(spot):
            acc[...] += lax.dot_general(
                hot, piece, (((1,), (1,)), ((), ())), preferred_element_type=F32
            )
        return carry

    lax.fori_loop(0, planes * chunks, cells, 0)
    wide_lane = lax.broadcasted_iota(jnp.int32, (high_blocks, 16 * LOW), 1)
    diagonal = jnp.zeros((high_blocks, 16 * LOW), F32)
    for r in range(16):
        inside = (wide_lane >= r * LOW) & (wide_lane < (r + 1) * LOW)
        diagonal = diagonal + jnp.where(inside, acc[r * high_blocks : (r + 1) * high_blocks, :], 0.0)
    folded = diagonal[:, :lanes] + diagonal[:, lanes:]
    for shift in (64, 32, 16):
        folded = folded + pltpu.roll(folded, shift, 1)
    grad_out[...] = folded
    for copy in spread(grad_out, grad_in, grad_s, grad_r, "slab", n, me):
        copy.wait()
    partial = total_of(grad_out[...], grad_in, n, me)
    grad_out2[...] = partial
    for copy in spread(grad_out2, grad_in2, grad2_s, grad2_r, "freq", nf, mine):
        copy.wait()
    gradient_ref[...] = total_of(partial, grad_in2, nf, mine)


def body(source, omega, sigma_blocks, block_ids, rec_owner, rec_edge, observed):
    n, nf = lax.axis_size("slab"), lax.axis_size("freq")
    planes, rows, lanes = block_ids.shape
    blocks = sigma_blocks.shape[0]
    high_blocks = blocks // LOW
    vmem = pl.BlockSpec(memory_space=pltpu.VMEM)
    smem = pl.BlockSpec(memory_space=pltpu.SMEM)
    cell = jax.ShapeDtypeStruct((planes, rows, lanes), F32)
    factor_real, factor_imag = pl.pallas_call(
        lookup_kernel,
        out_shape=(cell, cell),
        in_specs=[smem, vmem, vmem],
        out_specs=(vmem, vmem),
        name="lookup",
    )(omega, sigma_blocks.reshape(-1, lanes), block_ids)
    zero = jnp.zeros((lanes,), F32)
    pack = jnp.stack(
        [
            rec_owner[:, 0].astype(F32),
            (rec_edge >> 7).astype(F32),
            (rec_edge & 127).astype(F32),
            observed[0, 0],
            observed[0, 1],
            zero,
            zero,
            zero,
        ]
    )
    count = sum(1 if i == j else 2 for i, j in PAIRS)
    slots = 2 * SWEEPS
    cells_rows = 3 * planes * rows
    field = jax.ShapeDtypeStruct((2, 3, planes, rows, lanes), F32)
    halo = pltpu.VMEM((slots, 2, 2, rows, lanes), F32)
    dma = pltpu.SemaphoreType.DMA
    grad = pltpu.VMEM((high_blocks, lanes), F32)
    forward, adjoint, gradient = pl.pallas_call(
        functools.partial(kernel, n, nf, high_blocks),
        out_shape=(field, field, jax.ShapeDtypeStruct((high_blocks, lanes), F32)),
        in_specs=[smem, vmem, vmem, vmem, vmem, vmem],
        out_specs=(vmem, vmem, vmem),
        scratch_shapes=[
            pltpu.VMEM((SWEEPS + 1, 2, 3, planes, rows, lanes), F32),
            pltpu.VMEM((2, 3, planes, rows, lanes), F32),
            pltpu.VMEM((2, 2, planes, rows, lanes), F32),
            halo, halo, halo, halo,
            pltpu.VMEM((2, count, lanes), F32),
            pltpu.VMEM((2, n, count, lanes), F32),
            pltpu.VMEM((n, 8, lanes), F32),
            grad,
            pltpu.VMEM((n, high_blocks, lanes), F32),
            grad,
            pltpu.VMEM((nf, high_blocks, lanes), F32),
            pltpu.VMEM((lanes, cells_rows), BF16),
            pltpu.VMEM((cells_rows, n * lanes), BF16),
            pltpu.VMEM((cells_rows, 2 * lanes), BF16),
            pltpu.VMEM((cells_rows, 2 * lanes), BF16),
            pltpu.VMEM((n * lanes, 2 * lanes), BF16),
            pltpu.VMEM((n * lanes, 2 * lanes), BF16),
            pltpu.VMEM((16 * high_blocks, 16 * LOW), F32),
            dma((slots,)), dma((slots,)), dma((slots,)), dma((slots,)),
            dma((2, n)), dma((2, n)),
            dma((n,)), dma((n,)),
            dma((n,)), dma((n,)),
            dma((nf,)), dma((nf,)),
        ],
        compiler_params=pltpu.CompilerParams(
            collective_id=0, has_side_effects=True, vmem_limit_bytes=52 * 1024 * 1024
        ),
        name="solves",
    )(omega, source[0], factor_real, factor_imag, block_ids, pack)
    return forward[None], adjoint[None], gradient[:, :LOW].reshape(blocks)


def solution(mesh):
    return jax.shard_map(
        body,
        mesh=mesh,
        in_specs=(
            P("freq", None, None, "slab", None, None),
            P("freq"),
            P(),
            P("slab", None, None),
            P("slab", None),
            P("slab"),
            P("freq", None, "slab"),
        ),
        out_specs=(
            P("freq", None, None, "slab", None, None),
            P("freq", None, None, "slab", None, None),
            P(),
        ),
        check_vma=False,
    )
```

time: 1440 us -> 121 us (0.08)
  other arithmetic: 570 us -> 1.32 us
  local copies, waits for them, and re-layouts: 542 us -> 9.4 us
  blocking collectives: 202 us -> 0 us
  Pallas kernels: 0 us -> 108 us
  starting transfers between devices: 61 us -> 0 us
  waiting for transfers between devices: 35.1 us -> 0 us
  between operations: 18.4 us -> 1.29 us
    scatter-add x4 -> x0, other arithmetic: 500 us -> none  [the longest x1 453 us: body(): jax.ops.segment_sum(cell_term.reshape(-1), block_ids.reshape(-1), num_seg...]
    gather x5 -> x0, local copies, waits for them, and re-layouts: 415 us -> none  [the longest x1 406 us: body(): conductivity = jnp.take(sigma_blocks, block_ids, axis=0)]
    psum x9 -> x0, blocking collectives: 202 us -> none  [the longest x8 165 us: residual_sweeps(): lax.psum((jnp.sum(image_real * residual_real + image_imag * residual_imag...]
    pallas_call x0 -> x2, Pallas kernels: none -> 108 us  [the longest x1 105 us: body(): pl.pallas_call(functools.partial(kernel, n, nf, high_blocks), out_shape=(...]
    reshape x3 -> x1, local copies, waits for them, and re-layouts: 57.9 us -> 0.64 us  [body(): return (forward[None], adjoint[None], gradient[:, :LOW].reshape(blocks))]
    ppermute x16 -> x0, starting transfers between devices: 50.6 us -> none  [the longest x8 40.1 us: extended(): lax.ppermute(tail, axis, [(i, (i + 1) % count) for i in range(ends)])]
    add x1 -> x0, local copies, waits for them, and re-layouts: 44.4 us -> none  [residual_sweeps(): solution + jnp.stack([step_real * precond_real - step_imag * precond_imag...]
    sub x30 -> x0, other arithmetic: 28.7 us -> none  [the longest x6 21.2 us: residual_sweeps(): step_real * image_real - step_imag * image_imag]
  transfers between devices with their start and end apart: 19 -> 0, of which waited for: 15 -> 0; matrix products, arithmetic and copies ran while one was open for 1% -> 0% of each run, Pallas kernels for 0% -> 0%
where the time goes in v1:
time: 121 us; the launch traced here: 120 us
  Pallas kernels  108 us (89%)
  local copies, waits for them, and re-layouts  9.4 us (8%)
  other arithmetic  1.32 us (1%)
  between operations  1.29 us (1%)
    pallas_call x1, Pallas kernels, body(): pl.pallas_call(functools.partial(kernel, n, nf, high_blocks), out_shape=(...  105 us
    unnamed x12, local copies, waits for them, and re-layouts  7.97 us
    pallas_call x1, Pallas kernels, body(): pl.pallas_call(lookup_kernel, out_shape=(cell, cell), in_specs=[smem, vme...  3.41 us

profile of v1, /device:TPU:0, one launch (start us, length us, event | category | flops | bytes accessed | tf_op | source)
XLA Modules:
  0.0 120.3 jit_solution(12437471857368540301)
XLA Ops:
  1.3 0.7 convert_bitcast_fusion.2
  1.9 0.7 convert_bitcast_fusion
  2.6 0.8 slice_bitcast_fusion
  3.4 3.4 %lookup.1 = (f32[8,64,128]{2,1,0:T(8,128)}, f32[8,64,128]{2,1,0:T(8,128)}) custom-call(f32[1]{0:T(128)S(6)} %copy.12.omega_ref, f32[2,128]{1,0:T(2,128)} %bitcast.19, s32[8,64,128]{2,1,0:T(8,128)} %ids_ref.3), custom_call_target="tpu_custom_call" | custom-call | tf_op jit(solution)/shard_map/lookup/pallas_call | solution.py:408
  6.8 0.0 copy-start
  6.8 0.9 copy-done
  7.7 0.0 copy-start.1
  7.7 1.1 copy-done.1
  8.9 0.0 copy-start.2
  8.9 0.9 copy-done.2
  9.8 0.0 copy-start.3
  9.8 0.9 copy-done.3
  10.8 104.9 %solves.1 = (f32[2,3,8,64,128]{4,3,2,1,0:T(8,128)}, f32[2,3,8,64,128]{4,3,2,1,0:T(8,128)}, f32[16,128]{1,0:T(8,128)S(1)}) custom-call(f32[1]{0:T(128)S(6)} %copy.12.omega_ref, bf16[2,3,8,64,128]{4,3,2,1,0:T(8,128)(2,1)S(1)} %bitcast.15, f32[8,64,128]{2,1,0:T(8,128)S(1)} %copy-done.2, f32[8,64,128]{2,1,0:T(8,128)S(1)} %copy-done.3, ...), custom_call_target="tpu_custom_call" | custom-call | tf_op jit(solution)/shard_map/solves/pallas_call | solution.py:435
  115.6 0.6 reshape.24
  116.3 0.0 copy-start.4
  116.3 2.8 %copy.13 = f32[1,2,3,8,64,128]{5,4,3,2,1,0:T(8,128)} copy(f32[1,2,3,8,64,128]{5,4,3,2,1,0:T(8,128)} %bitcast.18) | data formatting | bytes 3145728
  119.1 0.0 copy-done.4
  119.1 1.1 copy.14
  (3 shorter events, 0.0 us)
Async XLA Ops:
  6.8 0.9 copy-start
  7.7 1.1 copy-start.1
  8.9 0.9 copy-start.2
  9.8 0.9 copy-start.3
  116.3 2.9 %copy-start.4 = (f32[2,3,8,64,128]{4,3,2,1,0:T(8,128)S(1)}, f32[2,3,8,64,128]{4,3,2,1,0:T(8,128)}, u32[]{:S(2)}) copy-start(f32[2,3,8,64,128]{4,3,2,1,0:T(8,128)} %get-tuple-element.11) | copy-start | bytes 4718596

commit v2 on v1

--- a/solution.py
+++ b/solution.py
@@ -13,10 +13,11 @@
 MESH = pl.DeviceIdType.MESH
 F32 = jnp.float32
 BF16 = jnp.bfloat16
-PAIRS = [(i, j) for i in range(SWEEPS + 1) for j in range(i, SWEEPS + 1) if j > 0]
-
-
-def lookup_kernel(omega_ref, sigma_ref, ids_ref, real_ref, imag_ref):
+PAIRS = [(i, j) for j in range(1, SWEEPS + 1) for i in range(j + 1)]
+WIDTH = SWEEPS
+
+
+def lookup_kernel(omega_ref, sigma_ref, ids_ref, damping_ref):
     planes, rows, lanes = ids_ref.shape
     tables = [jnp.broadcast_to(sigma_ref[k : k + 1, :], (8, lanes)) for k in range(sigma_ref.shape[0])]
     omega = omega_ref[0]
@@ -29,10 +30,7 @@
         value = jnp.take_along_axis(tables[0], low, axis=1)
         for k in range(1, len(tables)):
             value = jnp.where(high == k, jnp.take_along_axis(tables[k], low, axis=1), value)
-        damping = omega * value
-        inverse = 1.0 / (16.0 + damping * damping)
-        real_ref[x, pl.ds(y, 8), :] = 4.0 * inverse
-        imag_ref[x, pl.ds(y, 8), :] = damping * inverse
+        damping_ref[x, pl.ds(y, 8), :] = omega * value
         return carry
 
     lax.fori_loop(0, planes * per, step, 0, unroll=4)
@@ -45,18 +43,22 @@
 
 def kernel(
     n, nf, high_blocks,
-    omega_ref, source_ref, real_ref, imag_ref, ids_ref, pack_ref,
+    omega_ref, source_ref, damping_ref, ids_ref, owner_ref, edge_ref, observed_ref,
     forward_ref, adjoint_ref, gradient_ref,
+    real_ref, imag_ref, beside, pack_ref, mis_out, mis_in,
     basis, zb, curl, up_out, down_out, low_in, high_in,
     gram_out, gram_in, pack_in, grad_out, grad_in, grad_out2, grad_in2,
     rows_hot, rows_hot_t, field_hi, field_lo, mis_hi, mis_lo, acc,
     up_s, up_r, down_s, down_r, gram_s, gram_r, pack_s, pack_r, grad_s, grad_r, grad2_s, grad2_r,
+    near_s, near_r,
 ):
     me = lax.axis_index("slab")
     mine = lax.axis_index("freq")
-    planes, rows, lanes = real_ref.shape
-    last = planes - 1
+    planes, rows, lanes = damping_ref.shape
+    first, last = WIDTH, WIDTH + planes - 1
+    wide_planes = planes + 2 * WIDTH
     cells_rows = 3 * planes * rows
+    wide_rows = 3 * wide_planes * rows
 
     barrier = pltpu.get_barrier_semaphore()
     for d in range(1, n):
@@ -98,9 +100,50 @@
     def g2(v):
         return jnp.where(row == 0, 0.0, pltpu.roll(v, 1, 0)) - v
 
-    packs = spread(pack_ref, pack_in, pack_s, pack_r, "slab", n, me)
-    pack_in[0] = pack_ref[...]
+    edge = edge_ref[...]
+    blank = jnp.zeros((3, lanes), F32)
+    pack_ref[...] = jnp.concatenate(
+        [owner_ref[...].astype(F32), (edge >> 7).astype(F32), (edge & 127).astype(F32), observed_ref[...], blank],
+        axis=0,
+    )
+    packs = []
+    for d in range(1, n):
+        copy = pltpu.make_async_remote_copy(
+            src_ref=pack_ref, dst_ref=pack_in.at[me], send_sem=pack_s.at[d], recv_sem=pack_r.at[d],
+            device_id={"slab": lax.rem(me + d, n)}, device_id_type=MESH,
+        )
+        copy.start()
+        packs.append(copy)
+    pack_in[me] = pack_ref[...]
     valid = jnp.where(me > 0, 1.0, 0.0).astype(F32)
+
+    def factors(x, damping):
+        inverse = 1.0 / (16.0 + damping * damping)
+        real_ref[x] = 4.0 * inverse
+        imag_ref[x] = damping * inverse
+
+    def own_factors(x, carry):
+        factors(x + first, damping_ref[x])
+        for c in range(2):
+            for comp in range(3):
+                basis[0, c, comp, x + first] = source_ref[c, comp, x].astype(F32)
+        return carry
+
+    lax.fori_loop(0, planes, own_factors, 0)
+
+    def beside_copy(side):
+        begin, to = (planes - WIDTH, me + 1) if side == 0 else (0, me + n - 1)
+        return pltpu.make_async_remote_copy(
+            src_ref=damping_ref.at[pl.ds(begin, WIDTH)], dst_ref=beside.at[side], send_sem=near_s.at[side],
+            recv_sem=near_r.at[side], device_id={"slab": lax.rem(to, n)}, device_id_type=MESH,
+        )
+
+    def misfit_copy(side):
+        to = me + 1 if side == 0 else me + n - 1
+        return pltpu.make_async_remote_copy(
+            src_ref=mis_out, dst_ref=mis_in.at[side], send_sem=near_s.at[2 + side],
+            recv_sem=near_r.at[2 + side], device_id={"slab": lax.rem(to, n)}, device_id_type=MESH,
+        )
 
     def precondition(t, x):
         mr, mi = real_ref[x], imag_ref[x]
@@ -131,12 +174,17 @@
         basis[t + 1, c, 1, x] = b3p - b3 - g3(b1) - 4.0 * e2 + basis[t, c, 1, x]
         basis[t + 1, c, 2, x] = g2(b1) - (b2p - b2) - 4.0 * e3 + basis[t, c, 2, x]
 
-    def apply(first, t):
-        slot = first + t
-        precondition(t, 0)
+    def lower_curl(x):
         for c in range(2):
-            down_out[slot, c, 0] = zb[c, 1, 0]
-            down_out[slot, c, 1] = zb[c, 2, 0]
+            curl[c, 0, x] = f3(zb[c, 0, x]) - (zb[c, 2, x + 1] - zb[c, 2, x])
+            curl[c, 1, x] = zb[c, 1, x + 1] - zb[c, 1, x] - f2(zb[c, 0, x])
+
+    def apply(t, meanwhile):
+        slot = t
+        precondition(t, first)
+        for c in range(2):
+            down_out[slot, c, 0] = zb[c, 1, first]
+            down_out[slot, c, 1] = zb[c, 2, first]
 
         @pl.when(me > 0)
         def _():
@@ -155,17 +203,16 @@
             precondition(t, x)
             return carry
 
-        lax.fori_loop(1, last, inner, 0)
-        for c in range(2):
-            curl[c, 0, 0] = f3(zb[c, 0, 0]) - (zb[c, 2, 1] - zb[c, 2, 0])
-            curl[c, 1, 0] = zb[c, 1, 1] - zb[c, 1, 0] - f2(zb[c, 0, 0])
+        lax.fori_loop(first + 1, last, inner, 0)
+        lower_curl(first)
 
         def middle(x, carry):
             for c in range(2):
                 plane(t, c, x, zb[c, 1, x + 1], zb[c, 2, x + 1], curl[c, 0, x - 1], curl[c, 1, x - 1])
             return carry
 
-        lax.fori_loop(1, last, middle, 0)
+        lax.fori_loop(first + 1, last, middle, 0)
+        meanwhile()
 
         @pl.when(me > 0)
         def _():
@@ -178,9 +225,9 @@
 
         for c in range(2):
             plane(
-                t, c, 0, zb[c, 1, 1], zb[c, 2, 1],
-                (low_in[slot, c, 0] - zb[c, 2, 0]) * valid,
-                (zb[c, 1, 0] - low_in[slot, c, 1]) * valid,
+                t, c, first, zb[c, 1, first + 1], zb[c, 2, first + 1],
+                (low_in[slot, c, 0] - zb[c, 2, first]) * valid,
+                (zb[c, 1, first] - low_in[slot, c, 1]) * valid,
             )
 
         @pl.when(me < n - 1)
@@ -198,38 +245,68 @@
                 curl[c, 0, last - 1], curl[c, 1, last - 1],
             )
 
+    def apply_wide(t):
+        def inner(x, carry):
+            precondition(t, x)
+            return carry
+
+        lax.fori_loop(t, wide_planes - t, inner, 0)
+        lower_curl(t)
+
+        def middle(x, carry):
+            keep = jnp.where((x == first) & (me == 0), 0.0, 1.0).astype(F32)
+            for c in range(2):
+                plane(
+                    t, c, x, zb[c, 1, x + 1], zb[c, 2, x + 1],
+                    curl[c, 0, x - 1] * keep, curl[c, 1, x - 1] * keep,
+                )
+            return carry
+
+        lax.fori_loop(t + 1, wide_planes - t - 1, middle, 0)
+
     per = rows // 8
 
     def solve(which, out_ref):
-        def sweep(t, carry):
-            apply(which * SWEEPS, t)
-            return carry
-
-        lax.fori_loop(0, SWEEPS, sweep, 0)
-
-        def products(i, sums):
-            x, y = i // per, pl.multiple_of(i % per * 8, 8)
-            sums = list(sums)
-            for comp in range(3):
-                re = [basis[k, 0, comp, x, pl.ds(y, 8), :] for k in range(SWEEPS + 1)]
-                im = [basis[k, 1, comp, x, pl.ds(y, 8), :] for k in range(SWEEPS + 1)]
-                at = 0
-                for i_, j_ in PAIRS:
-                    sums[at] = sums[at] + (re[i_] * re[j_] + im[i_] * im[j_])
-                    at += 1
-                    if i_ != j_:
-                        sums[at] = sums[at] + (re[i_] * im[j_] - im[i_] * re[j_])
-                        at += 1
-            return tuple(sums)
-
-        count = gram_out.shape[1]
-        zero = jnp.zeros((8, lanes), F32)
-        sums = lax.fori_loop(0, planes * per, products, (zero,) * count)
-        for k in range(count):
-            gram_out[which, k : k + 1, :] = jnp.sum(sums[k], axis=0, keepdims=True)
+        def pair_sums(j_):
+            width = 2 * j_ + 1
+
+            def products(i, sums):
+                x, y = i // per + first, pl.multiple_of(i % per * 8, 8)
+                sums = list(sums)
+                for comp in range(3):
+                    re = [basis[k, 0, comp, x, pl.ds(y, 8), :] for k in range(j_ + 1)]
+                    im = [basis[k, 1, comp, x, pl.ds(y, 8), :] for k in range(j_ + 1)]
+                    for i_ in range(j_ + 1):
+                        sums[2 * i_] = sums[2 * i_] + (re[i_] * re[j_] + im[i_] * im[j_])
+                        if i_ != j_:
+                            sums[2 * i_ + 1] = sums[2 * i_ + 1] + (re[i_] * im[j_] - im[i_] * re[j_])
+                return tuple(sums)
+
+            zero = jnp.zeros((8, lanes), F32)
+            sums = lax.fori_loop(0, planes * per, products, (zero,) * width, unroll=2)
+            for k in range(width):
+                at = j_ * j_ - 1 + k
+                gram_out[which, at : at + 1, :] = jnp.sum(sums[k], axis=0, keepdims=True)
+
+        for t in range(SWEEPS):
+            if which == 0:
+                apply(t, functools.partial(pair_sums, t) if t else lambda: None)
+            else:
+                apply_wide(t)
+                if t:
+                    pair_sums(t)
+        pair_sums(SWEEPS)
         copies = spread(gram_out.at[which], gram_in.at[which], gram_s.at[which], gram_r.at[which], "slab", n, me)
         for copy in copies:
             copy.wait()
+        if which == 0:
+            @pl.when(me > 0)
+            def _():
+                beside_copy(1).start()
+
+            @pl.when(me < n - 1)
+            def _():
+                beside_copy(0).start()
         total = total_of(gram_out[which], gram_in.at[which], n, me)
         total = jnp.broadcast_to(jnp.sum(total, axis=1, keepdims=True), total.shape)
         gram, at = {}, 0
@@ -273,12 +350,12 @@
         wide = [(jnp.broadcast_to(a, (rows, lanes)), jnp.broadcast_to(b, (rows, lanes))) for a, b in coef]
 
         def combine(x, carry):
-            mr, mi = real_ref[x], imag_ref[x]
+            mr, mi = real_ref[x + first], imag_ref[x + first]
             for comp in range(3):
                 sr = jnp.zeros((rows, lanes), F32)
                 si = jnp.zeros((rows, lanes), F32)
                 for k in range(SWEEPS):
-                    br, bi = basis[k, 0, comp, x], basis[k, 1, comp, x]
+                    br, bi = basis[k, 0, comp, x + first], basis[k, 1, comp, x + first]
                     sr = sr + (wide[k][0] * br - wide[k][1] * bi)
                     si = si + (wide[k][0] * bi + wide[k][1] * br)
                 out_ref[0, comp, x] = mr * sr + mi * si
@@ -287,19 +364,13 @@
 
         lax.fori_loop(0, planes, combine, 0)
 
-    def load(x, carry):
-        for c in range(2):
-            for comp in range(3):
-                basis[0, c, comp, x] = source_ref[c, comp, x].astype(F32)
-        return carry
-
-    lax.fori_loop(0, planes, load, 0)
     solve(0, forward_ref)
 
     for copy in packs:
         copy.wait()
     self_id = me.astype(F32)
     blocks = cells_rows // lanes
+    wide_blocks = wide_rows // lanes
     for comp in range(3):
         for c in range(2):
             hi, lo = split(forward_ref[c, comp].reshape(planes * rows, lanes))
@@ -321,25 +392,93 @@
             rows_hot[:, k * lanes : (k + 1) * lanes] = jnp.where(
                 lane_sq == place - float(k * lanes), 1.0, 0.0
             ).astype(BF16)
-            rows_hot_t[k * lanes : (k + 1) * lanes, at] = jnp.where(
-                row_sq == owned[0:1, :] - float(k * lanes), 1.0, 0.0
-            ).astype(BF16)
         picked = jnp.dot(rows_hot[...], field_hi[...], preferred_element_type=F32)
         picked = picked + jnp.dot(rows_hot[...], field_lo[...], preferred_element_type=F32)
-        here = lane_sq == column[:, 1:2]
+        here = (lane_sq == column[:, 1:2]) & (place >= 0.0)
         re = jnp.where(here, picked[:, :lanes] - column[:, 2:3], 0.0)
         im = jnp.where(here, column[:, 3:4] - picked[:, lanes:], 0.0)
-        for part, values in enumerate((re, im)):
-            hi, lo = split(values)
+        both = jnp.where(
+            lane_sq == 0.0,
+            jnp.sum(re, axis=1, keepdims=True),
+            jnp.where(lane_sq == 1.0, jnp.sum(im, axis=1, keepdims=True), 0.0),
+        )
+        mis_out[d] = both.T[0:8, :]
+        return carry
+
+    lax.fori_loop(0, n, receivers, 0)
+
+    @pl.when(me > 0)
+    def _():
+        misfit_copy(1).start()
+
+    @pl.when(me < n - 1)
+    def _():
+        misfit_copy(0).start()
+
+    def places(p, carry):
+        at = pl.ds(pl.multiple_of(p * lanes, lanes), lanes)
+        pack = pack_in[p]
+        apart = pack[0:1, :] - self_id
+        number = pack[1:2, :].astype(jnp.int32)
+        comp = jnp.where(number >= 2 * planes * rows, 2, jnp.where(number >= planes * rows, 1, 0))
+        offset = (apart * float(planes * rows)).astype(jnp.int32) + WIDTH * rows
+        inside = number - comp * (planes * rows) + offset
+        fits = (inside >= 0) & (inside < wide_planes * rows)
+        spot = jnp.where(fits, inside + comp * (wide_planes * rows), -1).astype(F32)
+        for k in range(wide_blocks):
+            rows_hot_t[k * lanes : (k + 1) * lanes, at] = jnp.where(
+                row_sq == spot - float(k * lanes), 1.0, 0.0
+            ).astype(BF16)
+        return carry
+
+    lax.fori_loop(0, n, places, 0)
+
+    @pl.when(me > 0)
+    def _():
+        misfit_copy(0).wait_recv()
+        misfit_copy(1).wait_send()
+        beside_copy(0).wait_recv()
+        beside_copy(1).wait_send()
+
+    @pl.when(me < n - 1)
+    def _():
+        misfit_copy(1).wait_recv()
+        misfit_copy(0).wait_send()
+        beside_copy(1).wait_recv()
+        beside_copy(0).wait_send()
+
+    for side, there in enumerate((me > 0, me < n - 1)):
+        start = 0 if side == 0 else last + 1
+
+        @pl.when(there)
+        def _(side=side, start=start):
+            for k in range(WIDTH):
+                factors(start + k, beside[side, k])
+
+        @pl.when(jnp.logical_not(there))
+        def _(side=side, start=start):
+            mis_in[side] = jnp.zeros(mis_in.shape[1:], F32)
+            for k in range(WIDTH):
+                real_ref[start + k] = jnp.zeros((rows, lanes), F32)
+                imag_ref[start + k] = jnp.zeros((rows, lanes), F32)
+
+    def values_of(p, carry):
+        at = pl.ds(pl.multiple_of(p * lanes, lanes), lanes)
+        value = mis_out[p] + mis_in[0, p] + mis_in[1, p]
+        value = jnp.concatenate([value[0:2, :], pack_in[p][2:8, :]], axis=0)
+        column = jnp.concatenate([value] * (lanes // 8), axis=0).T
+        here = lane_sq == column[:, 2:3]
+        for part in range(2):
+            hi, lo = split(jnp.where(here, column[:, part : part + 1], 0.0))
             mis_hi[at, part * lanes : (part + 1) * lanes] = hi
             mis_lo[at, part * lanes : (part + 1) * lanes] = lo
         return carry
 
-    lax.fori_loop(0, n, receivers, 0)
+    lax.fori_loop(0, n, values_of, 0)
     group = 4
     for comp in range(3):
-        for x in range(0, planes, group):
-            begin = (comp * planes + x) * rows
+        for x in range(0, wide_planes, group):
+            begin = (comp * wide_planes + x) * rows
             hot = rows_hot_t[begin : begin + group * rows, :]
             added = jnp.dot(hot, mis_hi[...], preferred_element_type=F32)
             added = added + jnp.dot(hot, mis_lo[...], preferred_element_type=F32)
@@ -372,10 +511,10 @@
         spot = jnp.concatenate(
             [jnp.where(low[r : r + 1, :] == low_iota, value[r : r + 1, :], 0.0) for r in range(16)], axis=0
         )
-        for piece in split(spot):
-            acc[...] += lax.dot_general(
-                hot, piece, (((1,), (1,)), ((), ())), preferred_element_type=F32
-            )
+        acc[...] += lax.dot_general(
+            jnp.concatenate([hot, hot], axis=1), jnp.concatenate(split(spot), axis=1),
+            (((1,), (1,)), ((), ())), preferred_element_type=F32,
+        )
         return carry
 
     lax.fori_loop(0, planes * chunks, cells, 0)
@@ -405,29 +544,17 @@
     vmem = pl.BlockSpec(memory_space=pltpu.VMEM)
     smem = pl.BlockSpec(memory_space=pltpu.SMEM)
     cell = jax.ShapeDtypeStruct((planes, rows, lanes), F32)
-    factor_real, factor_imag = pl.pallas_call(
+    damping = pl.pallas_call(
         lookup_kernel,
-        out_shape=(cell, cell),
+        out_shape=cell,
         in_specs=[smem, vmem, vmem],
-        out_specs=(vmem, vmem),
+        out_specs=vmem,
         name="lookup",
     )(omega, sigma_blocks.reshape(-1, lanes), block_ids)
-    zero = jnp.zeros((lanes,), F32)
-    pack = jnp.stack(
-        [
-            rec_owner[:, 0].astype(F32),
-            (rec_edge >> 7).astype(F32),
-            (rec_edge & 127).astype(F32),
-            observed[0, 0],
-            observed[0, 1],
-            zero,
-            zero,
-            zero,
-        ]
-    )
     count = sum(1 if i == j else 2 for i, j in PAIRS)
-    slots = 2 * SWEEPS
+    slots = SWEEPS
     cells_rows = 3 * planes * rows
+    wide_planes = planes + 2 * WIDTH
     field = jax.ShapeDtypeStruct((2, 3, planes, rows, lanes), F32)
     halo = pltpu.VMEM((slots, 2, 2, rows, lanes), F32)
     dma = pltpu.SemaphoreType.DMA
@@ -435,12 +562,18 @@
     forward, adjoint, gradient = pl.pallas_call(
         functools.partial(kernel, n, nf, high_blocks),
         out_shape=(field, field, jax.ShapeDtypeStruct((high_blocks, lanes), F32)),
-        in_specs=[smem, vmem, vmem, vmem, vmem, vmem],
+        in_specs=[smem] + [vmem] * 6,
         out_specs=(vmem, vmem, vmem),
         scratch_shapes=[
-            pltpu.VMEM((SWEEPS + 1, 2, 3, planes, rows, lanes), F32),
-            pltpu.VMEM((2, 3, planes, rows, lanes), F32),
-            pltpu.VMEM((2, 2, planes, rows, lanes), F32),
+            pltpu.VMEM((wide_planes, rows, lanes), F32),
+            pltpu.VMEM((wide_planes, rows, lanes), F32),
+            pltpu.VMEM((2, WIDTH, rows, lanes), F32),
+            pltpu.VMEM((8, lanes), F32),
+            pltpu.VMEM((n, 8, lanes), F32),
+            pltpu.VMEM((2, n, 8, lanes), F32),
+            pltpu.VMEM((SWEEPS + 1, 2, 3, wide_planes, rows, lanes), F32),
+            pltpu.VMEM((2, 3, wide_planes, rows, lanes), F32),
+            pltpu.VMEM((2, 2, wide_planes, rows, lanes), F32),
             halo, halo, halo, halo,
             pltpu.VMEM((2, count, lanes), F32),
             pltpu.VMEM((2, n, count, lanes), F32),
@@ -450,7 +583,7 @@
             grad,
             pltpu.VMEM((nf, high_blocks, lanes), F32),
             pltpu.VMEM((lanes, cells_rows), BF16),
-            pltpu.VMEM((cells_rows, n * lanes), BF16),
+            pltpu.VMEM((3 * wide_planes * rows, n * lanes), BF16),
             pltpu.VMEM((cells_rows, 2 * lanes), BF16),
             pltpu.VMEM((cells_rows, 2 * lanes), BF16),
             pltpu.VMEM((n * lanes, 2 * lanes), BF16),
@@ -461,12 +594,16 @@
             dma((n,)), dma((n,)),
             dma((n,)), dma((n,)),
             dma((nf,)), dma((nf,)),
+            dma((4,)), dma((4,)),
         ],
         compiler_params=pltpu.CompilerParams(
             collective_id=0, has_side_effects=True, vmem_limit_bytes=52 * 1024 * 1024
         ),
         name="solves",
-    )(omega, source[0], factor_real, factor_imag, block_ids, pack)
+    )(
+        omega, source[0], damping, block_ids,
+        rec_owner.reshape(1, -1), rec_edge.reshape(1, -1), observed[0],
+    )
     return forward[None], adjoint[None], gradient[:, :LOW].reshape(blocks)
 
 

time: 121 us -> 109 us (0.901)
  Pallas kernels: 108 us -> 98.2 us
  other arithmetic: 1.32 us -> 0 us
    pallas_call x1, Pallas kernels: 105 us -> 95 us  [body(): pl.pallas_call(functools.partial(kernel, n, nf, high_blocks), out_shape=(...]
    unnamed x12 -> x16, local copies, waits for them, and re-layouts: 7.97 us -> 9.01 us
where the time goes in v2:
time: 109 us
  Pallas kernels  98.2 us (90%)
  local copies, waits for them, and re-layouts  9.65 us (9%)
  between operations  1.29 us (1%)
    pallas_call x1, Pallas kernels, body(): pl.pallas_call(functools.partial(kernel, n, nf, high_blocks), out_shape=(...  95 us
    unnamed x16, local copies, waits for them, and re-layouts  9.01 us
    pallas_call x1, Pallas kernels, body(): pl.pallas_call(lookup_kernel, out_shape=cell, in_specs=[smem, vmem, vmem]...  3.18 us

profile of v2, /device:TPU:0, one launch (start us, length us, event | category | flops | bytes accessed | tf_op | source)
XLA Modules:
  0.0 109.1 jit_solution(288637886197485134)
XLA Ops:
  1.3 3.2 %lookup.1.damping_ref = f32[8,64,128]{2,1,0:T(8,128)} custom-call(f32[1]{0:T(128)S(6)} %copy.12.omega_ref, f32[2,128]{1,0:T(2,128)} %bitcast.15, s32[8,64,128]{2,1,0:T(8,128)} %ids_ref.3), custom_call_target="tpu_custom_call" | custom-call | tf_op jit(solution)/shard_map/lookup/pallas_call | solution.py:547
  4.5 0.0 copy-start
  4.5 0.9 copy-done
  5.4 0.0 copy-start.1
  5.4 0.9 copy-done.1
  6.4 0.0 copy-start.2
  6.4 1.1 %copy-done.2 = bf16[1,2,3,8,64,128]{5,4,3,2,1,0:T(8,128)(2,1)S(1)} copy-done((bf16[1,2,3,8,64,128]{5,4,3,2,1,0:T(8,128)(2,1)S(1)}, bf16[1,2,3,8,64,128]{5,4,3,2,1,0:T(8,128)(2,1)}, u32[]{:S(2)}) %copy-start.2) | copy-done | bytes 786456
  7.5 0.0 copy-start.3
  7.5 0.7 copy-done.3
  8.2 0.0 copy-start.4
  8.2 0.7 copy-done.4
  8.8 0.0 copy-start.5
  8.8 0.7 copy-done.5
  9.5 95.0 %solves.1 = (f32[2,3,8,64,128]{4,3,2,1,0:T(8,128)}, f32[2,3,8,64,128]{4,3,2,1,0:T(8,128)}, f32[16,128]{1,0:T(8,128)S(1)}) custom-call(f32[1]{0:T(128)S(6)} %copy.12.omega_ref, bf16[2,3,8,64,128]{4,3,2,1,0:T(8,128)(2,1)S(1)} %bitcast.8, f32[8,64,128]{2,1,0:T(8,128)S(1)} %copy-done.1, s32[8,64,128]{2,1,0:T(8,128)S(1)} %copy-done, s32[1,128]{1,0:T(1,128)S(1)} %bitcast.11, ...), custom_call_target="tpu_custom_call" | custom-call | tf_op jit(solution)/shard_map/solves/pallas_call | solution.py:562
  104.5 0.6 reshape.21
  105.1 0.0 copy-start.6
  105.1 2.8 %copy.13 = f32[1,2,3,8,64,128]{5,4,3,2,1,0:T(8,128)} copy(f32[1,2,3,8,64,128]{5,4,3,2,1,0:T(8,128)} %bitcast.14) | data formatting | bytes 3145728
  108.0 0.0 copy-done.6
  108.0 1.1 %copy.14 = f32[1,2,3,8,64,128]{5,4,3,2,1,0:T(8,128)} copy(f32[1,2,3,8,64,128]{5,4,3,2,1,0:T(8,128)S(1)} %bitcast.13) | data formatting | bytes 3145728
Async XLA Ops:
  4.5 0.9 copy-start
  5.4 0.9 copy-start.1
  6.4 1.1 %copy-start.2 = (bf16[1,2,3,8,64,128]{5,4,3,2,1,0:T(8,128)(2,1)S(1)}, bf16[1,2,3,8,64,128]{5,4,3,2,1,0:T(8,128)(2,1)}, u32[]{:S(2)}) copy-start(bf16[1,2,3,8,64,128]{5,4,3,2,1,0:T(8,128)(2,1)} %param.7) | copy-start | bytes 2359300
  7.5 0.7 copy-start.3
  8.2 0.7 copy-start.4
  8.8 0.7 copy-start.5
  105.1 2.9 %copy-start.6 = (f32[2,3,8,64,128]{4,3,2,1,0:T(8,128)S(1)}, f32[2,3,8,64,128]{4,3,2,1,0:T(8,128)}, u32[]{:S(2)}) copy-start(f32[2,3,8,64,128]{4,3,2,1,0:T(8,128)} %get-tuple-element.7) | copy-start | bytes 4718596
